TPU v7x, 32 devices: a whole 2x2x4 slice. The times are simulated.
32 devices in a mesh: section: 4 (over y, core), ep: 8 (over z, x).
Axes of the slice: x: 2, y: 2, z: 4, core: 2. Of those that a mesh axis runs over, the one named last changes fastest.
Arguments:
- output_gradient: bfloat16 [4, 256, 7168], P('section', 'ep'), may hold values from -6 to 6
- expert_ids: int32 [4, 256, 8], P('section', 'ep'), may hold values from 0 to 255, as said below
- gate_weights: float32 [4, 256, 8], P('section', 'ep'), may hold values from 0.1 to 1
- stored_preactivations: bfloat16 [4, 192, 2, 1024], P('section', 'ep'), may hold values from -6 to 6
- w_gate: bfloat16 [8192, 7168], P('ep'), may hold values from -0.0625 to 0.0625
- w_up: bfloat16 [8192, 7168], P('ep'), may hold values from -0.0625 to 0.0625
- w_down: bfloat16 [8192, 7168], P('ep'), may hold values from -0.125 to 0.125
Outputs:
- passed_grad: bfloat16 [4, 256, 7168], P('section', 'ep')
- down_grad: bfloat16 [4, 8192, 7168], P('section', 'ep')
Inputs may be any that keep to these rules, and one draw needn't show every extreme that they name: `expert_ids`: A token's 8 ids differ. Ids below 4 name the window's experts; of one device's 32 tokens at most 3 name any one of them, and in every section one of them is named by exactly 3 tokens of every device.
All inputs are finite; a program needn't handle non-finite values.
Results may differ from a plain program's by a relative error of at most 0.0049.
Values may be sent and summed in bfloat16 or wider, within the bound.
A program may use at most 128 MiB of HBM per device.

v0:
```python
import jax
import jax.numpy as jnp
from jax import lax
from jax.sharding import PartitionSpec as P

EXPERTS = 4
SLOT = 3


def passed_along(value, axis, by):
    size = lax.axis_size(axis)
    pairs = [(i, i + by) for i in range(size) if 0 <= i + by < size]
    return lax.ppermute(value, axis, pairs)


def expert_step(row_block, pre_rows, w_gate, w_up, w_down):
    gate_pre = pre_rows[:, 0, :].astype(jnp.float32)
    up_pre = pre_rows[:, 1, :].astype(jnp.float32)
    sigmoid_gate = jax.nn.sigmoid(gate_pre)
    swish = gate_pre * sigmoid_gate
    d_hidden = lax.dot_general(
        row_block, w_down, (((1,), (1,)), ((), ())), preferred_element_type=jnp.float32
    )
    hidden = (swish * up_pre).astype(jnp.bfloat16)
    d_gate = (d_hidden * up_pre * sigmoid_gate * (1.0 + gate_pre * (1.0 - sigmoid_gate))).astype(
        jnp.bfloat16
    )
    d_up = (d_hidden * swish).astype(jnp.bfloat16)
    partial_terms = jnp.dot(d_gate, w_gate, preferred_element_type=jnp.float32)
    partial_terms = partial_terms + jnp.dot(d_up, w_up, preferred_element_type=jnp.float32)
    down_part = lax.dot_general(
        hidden, row_block, (((0,), (0,)), ((), ())), preferred_element_type=jnp.float32
    )
    return (partial_terms.astype(jnp.bfloat16), down_part)


def on_device(
    output_gradient, expert_ids, gate_weights, stored_preactivations, w_gate, w_up, w_down
):
    n_dev = lax.axis_size("ep")
    slices = n_dev // EXPERTS
    gradient = output_gradient[0]
    token_ids = expert_ids[0]
    token_gates = gate_weights[0]
    width = gradient.shape[1]
    hid_width = w_down.shape[0]
    matches = token_ids[:, :, None] == jnp.arange(EXPERTS, dtype=jnp.int32)
    members = jnp.sum(matches.astype(jnp.int32), axis=1)
    coefficient = jnp.sum(jnp.where(matches, token_gates[:, :, None], jnp.float32(0.0)), axis=1)
    ranking = jnp.cumsum(members, axis=0) - 1
    slot_ids = jnp.arange(SLOT, dtype=jnp.int32)[:, None, None]
    chosen = jnp.logical_and(members[None] == 1, ranking[None] == slot_ids)
    chosen = jnp.transpose(chosen, (2, 0, 1))
    picked = jnp.einsum(
        "ekt,td->ekd", chosen.astype(jnp.bfloat16), gradient, preferred_element_type=jnp.float32
    ).astype(jnp.bfloat16)
    outgoing = jnp.repeat(picked, slices, axis=0)
    saved_rows = stored_preactivations[0].reshape(n_dev, SLOT, 2, hid_width)
    relay_incoming = lax.all_to_all(outgoing, "ep", split_axis=0, concat_axis=0, tiled=True)
    partial_terms, down_part = expert_step(
        relay_incoming.reshape(n_dev * SLOT, width),
        saved_rows.reshape(n_dev * SLOT, 2, hid_width),
        w_gate,
        w_up,
        w_down,
    )
    returned = lax.all_to_all(
        partial_terms.reshape(n_dev, SLOT, width), "ep", split_axis=0, concat_axis=0, tiled=True
    )
    accumulated_total = jnp.sum(
        returned.reshape(EXPERTS, slices, SLOT, width), axis=1, dtype=jnp.float32
    )
    gate_weighting_factor = chosen.astype(jnp.float32) * jnp.transpose(coefficient)[:, None, :]
    expert_contribution = jnp.einsum(
        "ekt,ekd->td", gate_weighting_factor, accumulated_total, precision=lax.Precision.HIGHEST
    )
    grad_in = (gradient.astype(jnp.float32) + expert_contribution).astype(jnp.bfloat16)
    passed = passed_along(grad_in, "section", -1)
    return (passed[None], down_part.astype(jnp.bfloat16)[None])


def solution(mesh):
    placed = (
        P("section", "ep", None),
        P("section", "ep", None),
        P("section", "ep", None),
        P("section", "ep", None, None),
        P("ep", None),
        P("ep", None),
        P("ep", None),
    )
    return jax.shard_map(
        on_device,
        mesh=mesh,
        in_specs=placed,
        out_specs=(P("section", "ep", None), P("section", "ep", None)),
        check_vma=False,
    )
```

profile of v0, /device:TPU:1, one launch (start us, length us, event | category | flops | bytes accessed | tf_op | source)
XLA Modules:
  0.0 73.0 jit_solution(12955562842992190823)
XLA Ops:
  0.6 0.7 convert_reduce_fusion.1
  1.3 0.1 copy.28
  1.4 0.1 reduce_window_sum.11
  1.5 0.1 copy.29
  1.6 1.2 %convolution_convert_fusion = bf16[4,3,7168]{2,0,1:T(4,128)(2,1)S(1)} fusion(bf16[1,32,7168]{2,1,0:T(8,128)(2,1)} %param.7, s32[4,32]{1,0:T(4,128)S(1)} %copy.29, pred[4,32]{1,0:T(4,128)(4,1)S(1)} %compare_bitcast_fusion), kind=kOutput, calls=%fused_computation.6 | convolution fusion | flops 5591808 | bytes 631424 | tf_op jit(solution)/shard_map/ekt,td->ekd/dot_general | solution.py:54
  2.8 0.1 copy.30
  2.9 0.9 %broadcast_in_dim.31 = bf16[4,2,3,7168]{3,2,1,0:T(4,128)(2,1)} broadcast(bf16[4,3,7168]{2,1,0:T(4,128)(2,1)S(1)} %copy.30), dimensions={0,2,3} | broadcast | bytes 516096 | tf_op jit(solution)/shard_map/broadcast_in_dim | solution.py:57
  3.8 6.4 %all-to-all-start = ((bf16[8,3,7168]{2,1,0:T(4,128)(2,1)}), bf16[8,3,7168]{2,1,0:T(4,128)(2,1)S(1)}, u32[]{:S(2)}, u32[]{:S(2)}) async-start(bf16[8,3,7168]{2,1,0:T(4,128)(2,1)} %bitcast.7), calls=%async_computation | async-start | bytes 917504 | tf_op jit(solution)/shard_map/all_to_all | solution.py:59
  10.2 0.9 %copy.36 = bf16[1,24,2,1024]{3,1,2,0:T(8,128)(2,1)S(1)} copy(bf16[1,24,2,1024]{3,2,1,0:T(2,128)(2,1)} %param.10) | data formatting | bytes 196608 | tf_op args[3]
  11.1 11.3 %all-to-all-done = bf16[8,3,7168]{2,1,0:T(4,128)(2,1)S(1)} async-done(((bf16[8,3,7168]{2,1,0:T(4,128)(2,1)}), bf16[8,3,7168]{2,1,0:T(4,128)(2,1)S(1)}, u32[]{:S(2)}, u32[]{:S(2)}) %all-to-all-start) | async-done | bytes 344096 | tf_op jit(solution)/shard_map/all_to_all | solution.py:59
  22.4 0.3 reshape.36
  22.7 9.2 %fusion.48 = f32[24,1024]{1,0:T(8,128)S(1)} fusion(bf16[24,7168]{1,0:T(8,128)(2,1)S(1)} %reshape.36, bf16[1024,7168]{1,0:T(8,128)(2,1)} %param.13), kind=kOutput, calls=%fused_computation.60 | convolution fusion | flops 352321536 | bytes 15122432 | tf_op jit(solution)/shard_map/dot_general | solution.py:21
  31.9 0.0 slice-start.3
  31.9 7.4 %fusion.23 = f32[24,7168]{1,0:T(8,128)S(1)} fusion(bf16[1024,7168]{1,0:T(8,128)(2,1)} %param.11, f32[24,1024]{1,0:T(8,128)S(1)} %fusion.48, bf16[24,2,1024]{2,0,1:T(8,128)(2,1)S(1)} %bitcast.77), kind=kOutput, calls=%fused_computation.33 | convolution fusion | flops 352616448 | bytes 15564800 | tf_op jit(solution)/shard_map/dot_general | solution.py:29
  39.3 0.3 slice-done.3
  39.6 2.0 %fusion.2 = bf16[24,7168]{1,0:T(8,128)(2,1)S(1)} fusion(f32[24,7168]{1,0:T(8,128)S(1)} %fusion.23, bf16[1024,7168]{1,0:T(8,128)(2,1)S(1)} %bitcast.76, f32[24,1024]{1,0:T(8,128)S(1)} %fusion.48, bf16[24,2,1024]{2,0,1:T(8,128)(2,1)S(1)} %bitcast.78), kind=kOutput, calls=%fused_computation.5 | convolution fusion | flops 352837632 | bytes 15859712 | tf_op jit(solution)/shard_map/dot_general | solution.py:30
  41.6 1.0 %reshape.37 = bf16[8,3,7168]{2,1,0:T(4,128)(2,1)} reshape(bf16[24,7168]{1,0:T(8,128)(2,1)S(1)} %fusion.2) | data formatting | bytes 688128 | tf_op jit(solution)/shard_map/reshape | solution.py:68
  42.6 4.6 %all-to-all-start.1 = ((bf16[8,3,7168]{2,1,0:T(4,128)(2,1)}), bf16[8,3,7168]{2,1,0:T(4,128)(2,1)S(1)}, u32[]{:S(2)}, u32[]{:S(2)}) async-start(bf16[8,3,7168]{2,1,0:T(4,128)(2,1)} %reshape.37), calls=%async_computation.1 | async-start | bytes 917504 | tf_op jit(solution)/shard_map/all_to_all | solution.py:67
  47.3 12.2 %all-to-all-done.1 = bf16[8,3,7168]{2,1,0:T(4,128)(2,1)S(1)} async-done(((bf16[8,3,7168]{2,1,0:T(4,128)(2,1)}), bf16[8,3,7168]{2,1,0:T(4,128)(2,1)S(1)}, u32[]{:S(2)}, u32[]{:S(2)}) %all-to-all-start.1) | async-done | bytes 344096 | tf_op jit(solution)/shard_map/all_to_all | solution.py:67
  59.5 0.3 convert_reduce_fusion
  59.8 1.2 %fusion.1 = bf16[32,7168]{1,0:T(8,128)(2,1)S(1)} fusion(bf16[1,32,7168]{2,1,0:T(8,128)(2,1)S(1)} %copy-done, f32[4,3,7168]{2,1,0:T(4,128)S(1)} %convert_reduce_fusion, f32[4,32]{1,0:T(4,128)S(1)} %bitcast.84, s32[4,32]{1,0:T(4,128)S(1)} %copy.29, pred[4,32]{1,0:T(4,128)(4,1)S(1)} %compare_bitcast_fusion), kind=kOutput, calls=%fused_computation.3 | convolution fusion | flops 33719424 | bytes 1262720 | tf_op jit(solution)/shard_map/ekt,ekd->td/dot_general | solution.py:74
  61.0 3.7 %collective-permute-start = (bf16[32,7168]{1,0:T(8,128)(2,1)S(1)}, bf16[32,7168]{1,0:T(8,128)(2,1)S(1)}, u32[]{:S(2)}, u32[]{:S(2)}) collective-permute-start(bf16[32,7168]{1,0:T(8,128)(2,1)S(1)} %fusion.1), channel_id=1, source_target_pairs={{8,0},{16,8},{24,16},{9,1},{17,9},{25,17},{10,2},{18,10},{26,18},{... | collective-permute-start | bytes 1376264 | tf_op jit(solution)/shard_map/ppermute | solution.py:13
  64.7 7.6 %convert_bitcast_fusion = bf16[1,1024,7168]{2,1,0:T(8,128)(2,1)} fusion(bf16[24,7168]{1,0:T(8,128)(2,1)S(1)} %reshape.36, bf16[24,2,1024]{2,0,1:T(8,128)(2,1)S(1)} %bitcast.79), kind=kOutput, calls=%fused_computation | convolution fusion | flops 359858176 | bytes 15122432 | tf_op jit(solution)/shard_map/dot_general | solution.py:31
  72.3 0.8 %copy.38 = bf16[1,32,7168]{2,1,0:T(8,128)(2,1)} copy(bf16[1,32,7168]{2,1,0:T(8,128)(2,1)S(1)} %bitcast.80) | data formatting | bytes 917504
  (17 shorter events, 0.1 us)
Async XLA Ops:
  3.8 18.5 %all-to-all-start = ((bf16[8,3,7168]{2,1,0:T(4,128)(2,1)}), bf16[8,3,7168]{2,1,0:T(4,128)(2,1)S(1)}, u32[]{:S(2)}, u32[]{:S(2)}) async-start(bf16[8,3,7168]{2,1,0:T(4,128)(2,1)} %bitcast.7), calls=%async_computation | async-start | bytes 917504 | tf_op jit(solution)/shard_map/all_to_all | solution.py:59
  22.6 16.6 %slice-start = ((s8[14680064]{0:T(1024)(128)(4,1)}), s8[4194304]{0:T(1024)(128)(4,1)S(1)}, s32[]{:S(2)}) async-start(s8[14680064]{0:T(1024)(128)(4,1)} %bitcast.75), calls=%async_computation.2 | async-start | bytes 8388608
  22.7 16.6 %slice-start.1 = ((s8[14680064]{0:T(1024)(128)(4,1)}), s8[2097152]{0:T(1024)(128)(4,1)S(1)}, s32[]{:S(2)}) async-start(s8[14680064]{0:T(1024)(128)(4,1)} %bitcast.75), calls=%async_computation.3 | async-start | bytes 4194304
  31.9 7.4 %slice-start.2 = ((s8[14680064]{0:T(1024)(128)(4,1)}), s8[4194304]{0:T(1024)(128)(4,1)S(1)}, s32[]{:S(2)}) async-start(s8[14680064]{0:T(1024)(128)(4,1)} %bitcast.75), calls=%async_computation.4 | async-start | bytes 8388608
  31.9 7.7 %slice-start.3 = ((s8[14680064]{0:T(1024)(128)(4,1)}), s8[4194304]{0:T(1024)(128)(4,1)S(1)}, s32[]{:S(2)}) async-start(s8[14680064]{0:T(1024)(128)(4,1)} %bitcast.75), calls=%async_computation.5 | async-start | bytes 8388608
  39.6 7.7 %copy-start.1 = (s32[1,32,8]{1,2,0:T(8,128)S(1)}, s32[1,32,8]{1,2,0:T(8,128)}, u32[]{:S(2)}) copy-start(s32[1,32,8]{1,2,0:T(8,128)} %param.8) | copy-start | bytes 3076
  39.6 7.7 %copy-start.2 = (f32[1,32,8]{1,2,0:T(8,128)S(1)}, f32[1,32,8]{1,2,0:T(8,128)}, u32[]{:S(2)}) copy-start(f32[1,32,8]{1,2,0:T(8,128)} %param.9) | copy-start | bytes 3076
  39.6 20.2 %copy-start = (bf16[1,32,7168]{2,1,0:T(8,128)(2,1)S(1)}, bf16[1,32,7168]{2,1,0:T(8,128)(2,1)}, u32[]{:S(2)}) copy-start(bf16[1,32,7168]{2,1,0:T(8,128)(2,1)} %param.7) | copy-start | bytes 1376260
  42.6 16.9 %all-to-all-start.1 = ((bf16[8,3,7168]{2,1,0:T(4,128)(2,1)}), bf16[8,3,7168]{2,1,0:T(4,128)(2,1)S(1)}, u32[]{:S(2)}, u32[]{:S(2)}) async-start(bf16[8,3,7168]{2,1,0:T(4,128)(2,1)} %reshape.37), calls=%async_computation.1 | async-start | bytes 917504 | tf_op jit(solution)/shard_map/all_to_all | solution.py:67
  61.0 11.3 %collective-permute-start = (bf16[32,7168]{1,0:T(8,128)(2,1)S(1)}, bf16[32,7168]{1,0:T(8,128)(2,1)S(1)}, u32[]{:S(2)}, u32[]{:S(2)}) collective-permute-start(bf16[32,7168]{1,0:T(8,128)(2,1)S(1)} %fusion.1), channel_id=1, source_target_pairs={{8,0},{16,8},{24,16},{9,1},{17,9},{25,17},{10,2},{18,10},{26,18},{... | collective-permute-start | bytes 1376264 | tf_op jit(solution)/shard_map/ppermute | solution.py:13
where the time goes:
time: 73.5 us; the launch traced here: 73 us
  matrix products  28.7 us (39%)
  waiting for transfers between devices  23.5 us (32%)
  starting transfers between devices  14.7 us (20%)
  local copies, waits for them, and re-layouts  4.43 us (6%)
  other arithmetic  1.05 us (1%)
  between operations  0.74 us (1%)
    all_to_all x1, waiting for transfers between devices, on_device(): lax.all_to_all(partial_terms.reshape(n_dev, SLOT, width), 'ep', split_axi...  12.2 us
    all_to_all x1, waiting for transfers between devices, on_device(): lax.all_to_all(outgoing, 'ep', split_axis=0, concat_axis=0, tiled=True)  11.3 us
    dot_general x1, matrix products, expert_step(): lax.dot_general(row_block, w_down, (((1,), (1,)), ((), ())), preferred_el...  9.23 us
    dot_general x1, matrix products, expert_step(): lax.dot_general(hidden, row_block, (((0,), (0,)), ((), ())), preferred_el...  7.61 us
    dot_general x1, matrix products, expert_step(): partial_terms = jnp.dot(d_gate, w_gate, preferred_element_type=jnp.float32)  7.35 us
    all_to_all x1, starting transfers between devices, on_device(): lax.all_to_all(outgoing, 'ep', split_axis=0, concat_axis=0, tiled=True)  6.36 us
    all_to_all x1, starting transfers between devices, on_device(): lax.all_to_all(partial_terms.reshape(n_dev, SLOT, width), 'ep', split_axi...  4.63 us
    ppermute x1, starting transfers between devices, passed_along(): return lax.ppermute(value, axis, pairs)  3.67 us
  transfers between devices with their start and end apart: 3, of which 2 were waited for; matrix products, arithmetic and copies ran while one was open for 12% of the time, Pallas kernels for 0%

commit v1 on v0

v1 whole, which is shorter than its diff:
```python
import functools

import jax
import jax.numpy as jnp
from jax import lax
from jax.experimental import pallas as pl
from jax.experimental.pallas import tpu as pltpu
from jax.sharding import PartitionSpec as P

EXPERTS = 4
SLOT = 3
PAD = 4
FOLD = 4
ROWS = EXPERTS * PAD
WIDE = 256
F32 = jnp.float32
BF16 = jnp.bfloat16


def nt(a, b):
    return lax.dot_general(a, b, (((1,), (1,)), ((), ())), preferred_element_type=F32)


def tn(a, b):
    return lax.dot_general(a, b, (((0,), (0,)), ((), ())), preferred_element_type=F32)


def nn(a, b):
    return lax.dot_general(a, b, (((1,), (0,)), ((), ())), preferred_element_type=F32)


def iota(shape, dim):
    return lax.broadcasted_iota(jnp.int32, shape, dim)


def main_kernel(
    n_dev, n_sec, pieces,
    grad_ref, ids_ref, gates_ref, pre_ref, wg_hbm, wu_hbm, wd_hbm,
    passed_ref, rows_ref, hidden_ref,
    wg, wu, wd, gsend, grecv, part, xsend, xrecv, zsend, zrecv, gbuf, dh, fg, fu, dgate, dup,
    sel, whi, wlo, perm,
    wd_sem, wg_sem, wu_sem,
    gz_s, gz_r, gx_s, gx_r, rx_s, rx_r, rz_s, rz_r, ps_s, ps_r,
):
    slices = n_dev // EXPERTS
    tok = grad_ref.shape[1]
    w = WIDE
    cw = FOLD * w
    j = lax.axis_index("ep")
    s = lax.axis_index("section")
    e = lax.div(j, slices)
    g = lax.rem(j, slices)

    def cols(p):
        return pl.ds(pl.multiple_of(p * cw, cw), cw)

    def wcopy(hbm, vm, sem, p):
        return pltpu.make_async_copy(hbm.at[:, cols(p)], vm.at[:, cols(p)], sem.at[p])

    barrier = pltpu.get_barrier_semaphore()
    for d in range(1, EXPERTS):
        pl.semaphore_signal(barrier, inc=1, device_id={"ep": lax.rem(e + d, EXPERTS) * slices + g},
                            device_id_type=pl.DeviceIdType.MESH)
    for d in range(1, slices):
        pl.semaphore_signal(barrier, inc=1, device_id={"ep": e * slices + lax.rem(g + d, slices)},
                            device_id_type=pl.DeviceIdType.MESH)

    @pl.when(s > 0)
    def _():
        pl.semaphore_signal(barrier, inc=1, device_id={"section": s - 1},
                            device_id_type=pl.DeviceIdType.MESH)

    @pl.when(s < n_sec - 1)
    def _():
        pl.semaphore_signal(barrier, inc=1, device_id={"section": s + 1},
                            device_id_type=pl.DeviceIdType.MESH)

    def issue_down(p, c):
        wcopy(wd_hbm, wd, wd_sem, p).start()
        return c

    def issue_rest(p, c):
        wcopy(wg_hbm, wg, wg_sem, p).start()
        wcopy(wu_hbm, wu, wu_sem, p).start()
        return c

    lax.fori_loop(0, pieces, issue_down, 0)
    lax.fori_loop(0, pieces, issue_rest, 0)

    ids = ids_ref[0]
    gates = gates_ref[0]
    lane = iota((tok, 128), 1)
    member = jnp.zeros((tok, 128), F32)
    coef = jnp.zeros((tok, 128), F32)
    for c in range(ids.shape[1]):
        eq = ids[:, c:c + 1] == lane
        member = member + jnp.where(eq, 1.0, 0.0)
        coef = coef + jnp.where(eq, gates[:, c:c + 1], 0.0)
    tri = jnp.where(iota((tok, tok), 0) >= iota((tok, tok), 1), 1.0, 0.0).astype(BF16)
    rank = nn(tri, member.astype(BF16)) - 1.0
    rank = jnp.where(member == 1.0, rank, -1.0).astype(BF16)
    rank4 = jnp.concatenate([rank] * FOLD, axis=0)
    q = EXPERTS * FOLD * PAD
    qt = FOLD * tok
    i0 = iota((q, 128), 0)
    spread = jnp.where((i0 >> 4) == iota((q, 128), 1), 1.0, 0.0).astype(BF16)
    ri, rj = iota((q, qt), 0), iota((q, qt), 1)
    hit = jnp.logical_and(
        nt(spread, rank4) == (ri & 3).astype(F32),
        jnp.logical_and(((ri >> 2) & 3) == lax.div(rj, tok), (ri & 3) < SLOT),
    )
    sel[...] = jnp.where(hit, 1.0, 0.0).astype(BF16)
    ci, cj = iota((qt, q), 0), iota((qt, q), 1)
    hit_t = jnp.logical_and(
        nt(rank4, spread) == (cj & 3).astype(F32),
        jnp.logical_and(((cj >> 2) & 3) == lax.div(ci, tok), (cj & 3) < SLOT),
    )
    high = coef.astype(BF16)
    low = (coef - high.astype(F32)).astype(BF16)
    whi[...] = jnp.where(hit_t, nt(jnp.concatenate([high] * FOLD, axis=0), spread), 0.0).astype(BF16)
    wlo[...] = jnp.where(hit_t, nt(jnp.concatenate([low] * FOLD, axis=0), spread), 0.0).astype(BF16)
    fi, fj = iota((q, q), 0), iota((q, q), 1)
    perm[...] = jnp.where(
        jnp.logical_and(
            jnp.logical_and((fi >> 4) == ((fj >> 2) & 3), ((fi >> 2) & 3) == (fj >> 4)),
            (fi & 3) == (fj & 3),
        ),
        1.0, 0.0,
    ).astype(BF16)

    def z_copy(src, dst, ss, rs, p, d):
        to = lax.rem(e + d, EXPERTS)
        return pltpu.make_async_remote_copy(
            src_ref=src.at[p, pl.ds(pl.multiple_of(to * ROWS, ROWS), ROWS)],
            dst_ref=dst.at[p, pl.ds(pl.multiple_of(e * ROWS, ROWS), ROWS)],
            send_sem=ss.at[p, d - 1], recv_sem=rs.at[p, d - 1],
            device_id={"ep": to * slices + g}, device_id_type=pl.DeviceIdType.MESH)

    def z_wait(src, dst, ss, rs, p, d):
        frm = lax.rem(e + EXPERTS - d, EXPERTS)
        spot = pl.ds(pl.multiple_of(frm * ROWS, ROWS), ROWS)
        pltpu.make_async_remote_copy(
            src_ref=src.at[p, spot], dst_ref=dst.at[p, spot],
            send_sem=ss.at[p, d - 1], recv_sem=rs.at[p, d - 1],
            device_id={"ep": frm * slices + g}, device_id_type=pl.DeviceIdType.MESH).wait_recv()

    def gx_copy(p, d, row):
        at = rows_ref.at[pl.ds(pl.multiple_of(row * ROWS, ROWS), ROWS), cols(p)]
        return pltpu.make_async_remote_copy(
            src_ref=at, dst_ref=at, send_sem=gx_s.at[p, d - 1], recv_sem=gx_r.at[p, d - 1],
            device_id={"ep": e * slices + lax.rem(g + d, slices)},
            device_id_type=pl.DeviceIdType.MESH)

    def rx_copy(p, d):
        to = lax.rem(g + d, slices)
        return pltpu.make_async_remote_copy(
            src_ref=xsend.at[p, pl.ds(pl.multiple_of(to * ROWS, ROWS), ROWS)],
            dst_ref=xrecv.at[p, d - 1],
            send_sem=rx_s.at[p, d - 1], recv_sem=rx_r.at[p, d - 1],
            device_id={"ep": e * slices + to}, device_id_type=pl.DeviceIdType.MESH)

    def ps_copy(p):
        return pltpu.make_async_remote_copy(
            src_ref=gbuf.at[:, cols(p)], dst_ref=passed_ref.at[:, cols(p)],
            send_sem=ps_s.at[p], recv_sem=ps_r.at[p],
            device_id={"section": lax.rem(s + n_sec - 1, n_sec)},
            device_id_type=pl.DeviceIdType.MESH)

    mine = pl.ds(pl.multiple_of(e * ROWS, ROWS), ROWS)

    def pick(p, c):
        block = grad_ref[0, :, cols(p)]
        stack = jnp.concatenate([block[:, f * w:(f + 1) * w] for f in range(FOLD)], axis=0)
        gsend[p] = nn(sel[...], stack).astype(BF16)
        grecv[p, mine] = gsend[p, mine]
        return c

    lax.fori_loop(0, pieces, pick, 0)

    neighbours = lax.div(s + n_sec - 1, n_sec) + lax.div(2 * n_sec - 2 - s, n_sec)
    pl.semaphore_wait(barrier, EXPERTS - 1 + slices - 1 + neighbours)

    def send_rows(p, c):
        for d in range(1, EXPERTS):
            z_copy(gsend, grecv, gz_s, gz_r, p, d).start()
        return c

    lax.fori_loop(0, pieces, send_rows, 0)

    m = slices * ROWS
    r = n_dev * SLOT
    pi, pj = iota((m, r), 0), iota((m, r), 1)
    source = (((pi >> 2) & 3) * slices + (pi >> 4)) * SLOT + (pi & 3)
    order = jnp.where(jnp.logical_and(source == pj, (pi & 3) < SLOT), 1.0, 0.0).astype(BF16)
    a = nn(order, pre_ref[0, :, 0, :])
    u = nn(order, pre_ref[0, :, 1, :])
    sig = jax.nn.sigmoid(a)
    swish = a * sig
    hidden_ref[...] = (swish * u).astype(BF16)
    fg[...] = u * sig * (1.0 + a * (1.0 - sig))
    fu[...] = swish
    dh[...] = jnp.zeros_like(dh)

    @pl.when(s == n_sec - 1)
    def _():
        passed_ref[...] = jnp.zeros_like(passed_ref)

    lag = 2

    def gather(p, c):
        @pl.when(p < pieces)
        def _():
            for d in range(1, EXPERTS):
                z_wait(gsend, grecv, gz_s, gz_r, p, d)
            flat = nn(perm[...], grecv[p]).astype(BF16)
            rows_ref[pl.ds(pl.multiple_of(g * ROWS, ROWS), ROWS), cols(p)] = jnp.concatenate(
                [flat[f * ROWS:(f + 1) * ROWS] for f in range(FOLD)], axis=1)
            for d in range(1, slices):
                gx_copy(p, d, g).start()

        @pl.when(p >= lag)
        def _():
            t = p - lag
            for d in range(1, slices):
                gx_copy(t, d, lax.rem(g + slices - d, slices)).wait_recv()
            wcopy(wd_hbm, wd, wd_sem, t).wait()
            dh[...] += nt(rows_ref[:, cols(t)], wd[:, cols(t)])
        return c

    lax.fori_loop(0, pieces + lag, gather, 0)

    d_hidden = dh[...]
    dgate[...] = (d_hidden * fg[...]).astype(BF16)
    dup[...] = (d_hidden * fu[...]).astype(BF16)

    lag_x, lag_z = 1, 3

    def give_back(p, c):
        @pl.when(p < pieces)
        def _():
            wcopy(wg_hbm, wg, wg_sem, p).wait()
            wcopy(wu_hbm, wu, wu_sem, p).wait()
            total = nn(dgate[...], wg[:, cols(p)]) + nn(dup[...], wu[:, cols(p)])
            xsend[p] = total.astype(BF16)
            for d in range(1, slices):
                rx_copy(p, d).start()

        @pl.when(jnp.logical_and(p >= lag_x, p < pieces + lag_x))
        def _():
            t = p - lag_x
            acc = xsend[t, pl.ds(pl.multiple_of(g * ROWS, ROWS), ROWS)].astype(F32)
            for d in range(1, slices):
                rx_copy(t, d).wait_recv()
                acc = acc + xrecv[t, d - 1].astype(F32)
            acc = acc.astype(BF16)
            stack = jnp.concatenate([acc[:, f * w:(f + 1) * w] for f in range(FOLD)], axis=0)
            zsend[t] = nn(perm[...], stack).astype(BF16)
            for d in range(1, EXPERTS):
                z_copy(zsend, zrecv, rz_s, rz_r, t, d).start()
            zrecv[t, mine] = zsend[t, mine]

        @pl.when(p >= lag_z)
        def _():
            t = p - lag_z
            for d in range(1, EXPERTS):
                z_wait(zsend, zrecv, rz_s, rz_r, t, d)
            got = zrecv[t]
            terms = nn(whi[...], got) + nn(wlo[...], got)
            wide = jnp.concatenate([terms[f * tok:(f + 1) * tok] for f in range(FOLD)], axis=1)
            gbuf[:, cols(t)] = (grad_ref[0, :, cols(t)].astype(F32) + wide).astype(BF16)

            @pl.when(s > 0)
            def _():
                ps_copy(t).start()
        return c

    lax.fori_loop(0, pieces + lag_z, give_back, 0)

    def drain(p, c):
        for d in range(1, EXPERTS):
            z_copy(gsend, grecv, gz_s, gz_r, p, d).wait_send()
            z_copy(zsend, zrecv, rz_s, rz_r, p, d).wait_send()
        for d in range(1, slices):
            gx_copy(p, d, g).wait_send()
            rx_copy(p, d).wait_send()

        @pl.when(s < n_sec - 1)
        def _():
            ps_copy(p).wait_recv()

        @pl.when(s > 0)
        def _():
            ps_copy(p).wait_send()
        return c

    lax.fori_loop(0, pieces, drain, 0)


def down_kernel(hidden_ref, rows_ref, passed_ref, down_ref, out_ref):
    @pl.when(pl.program_id(0) == 0)
    def _():
        out_ref[...] = passed_ref[...]

    step = FOLD * WIDE
    h = hidden_ref[...]
    for c in range(rows_ref.shape[1] // step):
        down_ref[:, c * step:(c + 1) * step] = tn(h, rows_ref[:, c * step:(c + 1) * step]).astype(BF16)


def on_device(grad, ids, gates, pre, w_gate, w_up, w_down):
    n_dev = lax.axis_size("ep")
    n_sec = lax.axis_size("section")
    slices = n_dev // EXPERTS
    tok, width = grad.shape[1:]
    hid = w_down.shape[0]
    pieces = width // (FOLD * WIDE)
    m = slices * ROWS
    q = EXPERTS * FOLD * PAD
    qt = FOLD * tok
    vmem = pl.BlockSpec(memory_space=pltpu.VMEM)
    hbm = pl.BlockSpec(memory_space=pl.ANY)
    dma = pltpu.SemaphoreType.DMA
    x_n = slices - 1
    z_n = EXPERTS - 1
    passed, rows, hidden = pl.pallas_call(
        functools.partial(main_kernel, n_dev, n_sec, pieces),
        out_shape=(
            jax.ShapeDtypeStruct((tok, width), BF16),
            jax.ShapeDtypeStruct((m, width), BF16),
            jax.ShapeDtypeStruct((m, hid), BF16),
        ),
        in_specs=[vmem, vmem, vmem, vmem, hbm, hbm, hbm],
        out_specs=(vmem, vmem, vmem),
        scratch_shapes=[
            pltpu.VMEM((hid, width), BF16),
            pltpu.VMEM((hid, width), BF16),
            pltpu.VMEM((hid, width), BF16),
            pltpu.VMEM((pieces, q, WIDE), BF16),
            pltpu.VMEM((pieces, q, WIDE), BF16),
            pltpu.VMEM((8, 128), F32),
            pltpu.VMEM((pieces, m, FOLD * WIDE), BF16),
            pltpu.VMEM((pieces, x_n, ROWS, FOLD * WIDE), BF16),
            pltpu.VMEM((pieces, q, WIDE), BF16),
            pltpu.VMEM((pieces, q, WIDE), BF16),
            pltpu.VMEM((tok, width), BF16),
            pltpu.VMEM((m, hid), F32),
            pltpu.VMEM((m, hid), F32),
            pltpu.VMEM((m, hid), F32),
            pltpu.VMEM((m, hid), BF16),
            pltpu.VMEM((m, hid), BF16),
            pltpu.VMEM((q, qt), BF16),
            pltpu.VMEM((qt, q), BF16),
            pltpu.VMEM((qt, q), BF16),
            pltpu.VMEM((q, q), BF16),
            dma((pieces,)), dma((pieces,)), dma((pieces,)),
            dma((pieces, z_n)), dma((pieces, z_n)),
            dma((pieces, x_n)), dma((pieces, x_n)),
            dma((pieces, x_n)), dma((pieces, x_n)),
            dma((pieces, z_n)), dma((pieces, z_n)),
            dma((pieces,)), dma((pieces,)),
        ],
        compiler_params=pltpu.CompilerParams(
            collective_id=0, has_side_effects=True, vmem_limit_bytes=60 * 1024 * 1024),
        cost_estimate=pl.CostEstimate(
            flops=6 * m * hid * width, bytes_accessed=6 * hid * width, transcendentals=m * hid),
    )(grad, ids, gates, pre, w_gate, w_up, w_down)
    block = min(hid, 256)
    down, out = pl.pallas_call(
        down_kernel,
        grid=(hid // block,),
        out_shape=(
            jax.ShapeDtypeStruct((hid, width), BF16),
            jax.ShapeDtypeStruct((tok, width), BF16),
        ),
        in_specs=[
            pl.BlockSpec((m, block), lambda i: (0, i)),
            pl.BlockSpec((m, width), lambda i: (0, 0)),
            pl.BlockSpec((tok, width), lambda i: (0, 0)),
        ],
        out_specs=(
            pl.BlockSpec((block, width), lambda i: (i, 0)),
            pl.BlockSpec((tok, width), lambda i: (0, 0)),
        ),
        compiler_params=pltpu.CompilerParams(vmem_limit_bytes=48 * 1024 * 1024),
        cost_estimate=pl.CostEstimate(
            flops=2 * m * hid * width, bytes_accessed=2 * hid * width, transcendentals=0),
    )(hidden, rows, passed)
    return (out[None], down[None])


def solution(mesh):
    placed = (
        P("section", "ep", None),
        P("section", "ep", None),
        P("section", "ep", None),
        P("section", "ep", None, None),
        P("ep", None),
        P("ep", None),
        P("ep", None),
    )
    return jax.shard_map(
        on_device,
        mesh=mesh,
        in_specs=placed,
        out_specs=(P("section", "ep", None), P("section", "ep", None)),
        check_vma=False,
    )
```

time: 73.5 us -> 61 us (0.83)
  Pallas kernels: 0 us -> 54.5 us
  matrix products: 28.7 us -> 0 us
  waiting for transfers between devices: 23.5 us -> 0 us
  starting transfers between devices: 14.7 us -> 0 us
  local copies, waits for them, and re-layouts: 4.43 us -> 5.6 us
  other arithmetic: 1.05 us -> 0 us
    pallas_call x0 -> x2, Pallas kernels: none -> 54.5 us  [the longest x1 47.2 us: on_device(): pl.pallas_call(functools.partial(main_kernel, n_dev, n_sec, pieces), out_...]
    dot_general x6 -> x0, matrix products: 28.7 us -> none  [the longest x1 9.23 us: expert_step(): lax.dot_general(row_block, w_down, (((1,), (1,)), ((), ())), preferred_el...]
    all_to_all x2 -> x0, waiting for transfers between devices: 23.5 us -> none  [the longest x1 12.2 us: on_device(): lax.all_to_all(partial_terms.reshape(n_dev, SLOT, width), 'ep', split_axi...]
    all_to_all x2 -> x0, starting transfers between devices: 11 us -> none  [the longest x1 6.36 us: on_device(): lax.all_to_all(outgoing, 'ep', split_axis=0, concat_axis=0, tiled=True)]
    ppermute x1 -> x0, starting transfers between devices: 3.67 us -> none  [passed_along(): return lax.ppermute(value, axis, pairs)]
    unnamed x16 -> x8, local copies, waits for them, and re-layouts: 1.98 us -> 5.6 us
    reshape x2 -> x0, local copies, waits for them, and re-layouts: 1.28 us -> none  [the longest x1 0.99 us: on_device(): partial_terms.reshape(n_dev, SLOT, width)]
    reduce_sum x3 -> x0, other arithmetic: 0.98 us -> none  [the longest x1 0.71 us: on_device(): members = jnp.sum(matches.astype(jnp.int32), axis=1)]
  transfers between devices with their start and end apart: 3 -> 0, of which waited for: 2 -> 0; matrix products, arithmetic and copies ran while one was open for 12% -> 0% of each run, Pallas kernels for 0% -> 0%
where the time goes in v1:
time: 61 us; the launch traced here: 60.7 us
  Pallas kernels  54.5 us (89%)
  local copies, waits for them, and re-layouts  5.6 us (9%)
  between operations  0.65 us (1%)
    pallas_call x1, Pallas kernels, on_device(): pl.pallas_call(functools.partial(main_kernel, n_dev, n_sec, pieces), out_...  47.2 us
    pallas_call x1, Pallas kernels, on_device(): pl.pallas_call(down_kernel, grid=(hid // block,), out_shape=(jax.ShapeDty...  7.22 us
    unnamed x8, local copies, waits for them, and re-layouts  5.6 us

profile of v1, /device:TPU:1, one launch (start us, length us, event | category | flops | bytes accessed | tf_op | source)
XLA Modules:
  0.0 60.7 jit_solution(17750738842143885392)
XLA Ops:
  0.6 1.4 %copy.9.ids_ref = s32[1,32,8]{2,1,0:T(8,128)} copy(s32[1,32,8]{1,2,0:T(8,128)} %param.8) | data formatting | bytes 2048 | tf_op args[1]
  2.0 1.4 %copy.10.gates_ref = f32[1,32,8]{2,1,0:T(8,128)} copy(f32[1,32,8]{1,2,0:T(8,128)} %param.9) | data formatting | bytes 2048 | tf_op args[2]
  3.4 47.2 %shard_map.86 = (bf16[32,7168]{1,0:T(8,128)(2,1)}, bf16[32,7168]{1,0:T(8,128)(2,1)}, bf16[32,1024]{1,0:T(8,128)(2,1)}) custom-call(bf16[1,32,7168]{2,1,0:T(8,128)(2,1)} %grad_ref.1, s32[1,32,8]{2,1,0:T(8,128)} %copy.9.ids_ref, f32[1,32,8]{2,1,0:T(8,128)} %copy.10.gates_ref, bf16[1,24,2,1024]{3,2,1,0:T(2,128)(2,1)} %pre_ref.1, bf16[1024,7168]{1,0:T(8,128)(2,1)} %wg_hbm.1, ...), custom_call_target="tpu_custom_call" | custom-call | flops 1409286144 | bytes 44040192 | tf_op jit(solution)/shard_map/pallas_call | solution.py:325
  50.6 0.0 copy-start
  50.6 1.0 %copy-done = bf16[32,7168]{1,0:T(8,128)(2,1)S(1)} copy-done((bf16[32,7168]{1,0:T(8,128)(2,1)S(1)}, bf16[32,7168]{1,0:T(8,128)(2,1)}, u32[]{:S(2)}) %copy-start) | copy-done | bytes 458776
  51.6 0.0 copy-start.1
  51.6 1.0 %copy-done.1 = bf16[32,7168]{1,0:T(8,128)(2,1)S(1)} copy-done((bf16[32,7168]{1,0:T(8,128)(2,1)S(1)}, bf16[32,7168]{1,0:T(8,128)(2,1)}, u32[]{:S(2)}) %copy-start.1) | copy-done | bytes 458776
  52.6 0.0 copy-start.2
  52.6 0.8 %copy-done.2 = bf16[32,1024]{1,0:T(8,128)(2,1)S(1)} copy-done((bf16[32,1024]{1,0:T(8,128)(2,1)S(1)}, bf16[32,1024]{1,0:T(8,128)(2,1)}, u32[]{:S(2)}) %copy-start.2) | copy-done | bytes 65560
  53.5 7.2 %shard_map.87 = (bf16[1024,7168]{1,0:T(8,128)(2,1)}, bf16[32,7168]{1,0:T(8,128)(2,1)}) custom-call(bf16[32,1024]{1,0:T(8,128)(2,1)S(1)} %copy-done.2, bf16[32,7168]{1,0:T(8,128)(2,1)S(1)} %copy-done.1, bf16[32,7168]{1,0:T(8,128)(2,1)S(1)} %copy-done), custom_call_target="tpu_custom_call" | custom-call | flops 469762048 | bytes 14680064 | tf_op jit(solution)/shard_map/pallas_call | solution.py:368
Async XLA Ops:
  50.6 1.0 %copy-start = (bf16[32,7168]{1,0:T(8,128)(2,1)S(1)}, bf16[32,7168]{1,0:T(8,128)(2,1)}, u32[]{:S(2)}) copy-start(bf16[32,7168]{1,0:T(8,128)(2,1)} %get-tuple-element.9.passed_ref) | copy-start | bytes 1376260
  51.6 1.0 %copy-start.1 = (bf16[32,7168]{1,0:T(8,128)(2,1)S(1)}, bf16[32,7168]{1,0:T(8,128)(2,1)}, u32[]{:S(2)}) copy-start(bf16[32,7168]{1,0:T(8,128)(2,1)} %get-tuple-element.8.rows_ref) | copy-start | bytes 1376260
  52.6 0.8 %copy-start.2 = (bf16[32,1024]{1,0:T(8,128)(2,1)S(1)}, bf16[32,1024]{1,0:T(8,128)(2,1)}, u32[]{:S(2)}) copy-start(bf16[32,1024]{1,0:T(8,128)(2,1)} %get-tuple-element.7.hidden_ref) | copy-start | bytes 196612

commit v2 on v1

--- a/solution.py
+++ b/solution.py
@@ -12,7 +12,7 @@
 PAD = 4
 FOLD = 4
 ROWS = EXPERTS * PAD
-WIDE = 256
+WIDE = 896
 F32 = jnp.float32
 BF16 = jnp.bfloat16
 
@@ -37,7 +37,7 @@
     n_dev, n_sec, pieces,
     grad_ref, ids_ref, gates_ref, pre_ref, wg_hbm, wu_hbm, wd_hbm,
     passed_ref, rows_ref, hidden_ref,
-    wg, wu, wd, gsend, grecv, part, xsend, xrecv, zsend, zrecv, gbuf, dh, fg, fu, dgate, dup,
+    wg, wu, wd, gsend, grecv, xsend, xrecv, zsend, zrecv, gbuf, dh, fg, fu, dgate, dup,
     sel, whi, wlo, perm,
     wd_sem, wg_sem, wu_sem,
     gz_s, gz_r, gx_s, gx_r, rx_s, rx_r, rz_s, rz_r, ps_s, ps_r,
@@ -89,36 +89,39 @@
 
     ids = ids_ref[0]
     gates = gates_ref[0]
-    lane = iota((tok, 128), 1)
-    member = jnp.zeros((tok, 128), F32)
-    coef = jnp.zeros((tok, 128), F32)
-    for c in range(ids.shape[1]):
-        eq = ids[:, c:c + 1] == lane
-        member = member + jnp.where(eq, 1.0, 0.0)
-        coef = coef + jnp.where(eq, gates[:, c:c + 1], 0.0)
-    tri = jnp.where(iota((tok, tok), 0) >= iota((tok, tok), 1), 1.0, 0.0).astype(BF16)
-    rank = nn(tri, member.astype(BF16)) - 1.0
-    rank = jnp.where(member == 1.0, rank, -1.0).astype(BF16)
-    rank4 = jnp.concatenate([rank] * FOLD, axis=0)
     q = EXPERTS * FOLD * PAD
     qt = FOLD * tok
-    i0 = iota((q, 128), 0)
-    spread = jnp.where((i0 >> 4) == iota((q, 128), 1), 1.0, 0.0).astype(BF16)
+    named = iota((ROWS, tok), 0)
+    member = jnp.zeros((ROWS, tok), F32)
+    coef = jnp.zeros((ROWS, tok), F32)
+    for c in range(ids.shape[0]):
+        eq = ids[c:c + 1, :] == named
+        member = member + jnp.where(eq, 1.0, 0.0)
+        coef = coef + jnp.where(eq, gates[c:c + 1, :], 0.0)
+    tri = jnp.where(iota((tok, tok), 0) <= iota((tok, tok), 1), 1.0, 0.0).astype(BF16)
+    rank = nn(member.astype(BF16), tri) - 1.0
+    rank = jnp.where(member == 1.0, rank, -1.0).astype(BF16)
+    tile = jnp.where(iota((tok, qt), 0) == lax.rem(iota((tok, qt), 1), tok), 1.0, 0.0).astype(BF16)
+    rank4 = nn(rank, tile).astype(BF16)
+    spread = jnp.where((iota((q, ROWS), 0) >> 4) == iota((q, ROWS), 1), 1.0, 0.0).astype(BF16)
+    spread_t = jnp.where(iota((ROWS, q), 0) == (iota((ROWS, q), 1) >> 4), 1.0, 0.0).astype(BF16)
     ri, rj = iota((q, qt), 0), iota((q, qt), 1)
     hit = jnp.logical_and(
-        nt(spread, rank4) == (ri & 3).astype(F32),
+        nn(spread, rank4) == (ri & 3).astype(F32),
         jnp.logical_and(((ri >> 2) & 3) == lax.div(rj, tok), (ri & 3) < SLOT),
     )
     sel[...] = jnp.where(hit, 1.0, 0.0).astype(BF16)
     ci, cj = iota((qt, q), 0), iota((qt, q), 1)
     hit_t = jnp.logical_and(
-        nt(rank4, spread) == (cj & 3).astype(F32),
+        tn(rank4, spread_t) == (cj & 3).astype(F32),
         jnp.logical_and(((cj >> 2) & 3) == lax.div(ci, tok), (cj & 3) < SLOT),
     )
     high = coef.astype(BF16)
     low = (coef - high.astype(F32)).astype(BF16)
-    whi[...] = jnp.where(hit_t, nt(jnp.concatenate([high] * FOLD, axis=0), spread), 0.0).astype(BF16)
-    wlo[...] = jnp.where(hit_t, nt(jnp.concatenate([low] * FOLD, axis=0), spread), 0.0).astype(BF16)
+    high4 = nn(high, tile).astype(BF16)
+    low4 = nn(low, tile).astype(BF16)
+    whi[...] = jnp.where(hit_t, tn(high4, spread_t), 0.0).astype(BF16)
+    wlo[...] = jnp.where(hit_t, tn(low4, spread_t), 0.0).astype(BF16)
     fi, fj = iota((q, q), 0), iota((q, q), 1)
     perm[...] = jnp.where(
         jnp.logical_and(
@@ -337,7 +340,6 @@
             pltpu.VMEM((hid, width), BF16),
             pltpu.VMEM((pieces, q, WIDE), BF16),
             pltpu.VMEM((pieces, q, WIDE), BF16),
-            pltpu.VMEM((8, 128), F32),
             pltpu.VMEM((pieces, m, FOLD * WIDE), BF16),
             pltpu.VMEM((pieces, x_n, ROWS, FOLD * WIDE), BF16),
             pltpu.VMEM((pieces, q, WIDE), BF16),
@@ -363,8 +365,8 @@
             collective_id=0, has_side_effects=True, vmem_limit_bytes=60 * 1024 * 1024),
         cost_estimate=pl.CostEstimate(
             flops=6 * m * hid * width, bytes_accessed=6 * hid * width, transcendentals=m * hid),
-    )(grad, ids, gates, pre, w_gate, w_up, w_down)
-    block = min(hid, 256)
+    )(grad, jnp.swapaxes(ids, 1, 2), jnp.swapaxes(gates, 1, 2), pre, w_gate, w_up, w_down)
+    block = min(hid, 128)
     down, out = pl.pallas_call(
         down_kernel,
         grid=(hid // block,),
@@ -381,7 +383,7 @@
             pl.BlockSpec((block, width), lambda i: (i, 0)),
             pl.BlockSpec((tok, width), lambda i: (0, 0)),
         ),
-        compiler_params=pltpu.CompilerParams(vmem_limit_bytes=48 * 1024 * 1024),
+        compiler_params=pltpu.CompilerParams(vmem_limit_bytes=60 * 1024 * 1024),
         cost_estimate=pl.CostEstimate(
             flops=2 * m * hid * width, bytes_accessed=2 * hid * width, transcendentals=0),
     )(hidden, rows, passed)

time: 61 us -> 50.1 us (0.82)
  local copies, waits for them, and re-layouts: 5.6 us -> 0 us
  Pallas kernels: 54.5 us -> 49.1 us
    pallas_call x1, Pallas kernels: 47.2 us -> 39.6 us  [on_device(): pl.pallas_call(functools.partial(main_kernel, n_dev, n_sec, pieces), out_...]
    unnamed x8 -> x0, local copies, waits for them, and re-layouts: 5.6 us -> none
    pallas_call x1, Pallas kernels: 7.22 us -> 9.51 us  [on_device(): pl.pallas_call(down_kernel, grid=(hid // block,), out_shape=(jax.ShapeDty...]
where the time goes in v2:
time: 50.1 us; the launch traced here: 49.8 us
  Pallas kernels  49.1 us (98%)
  between operations  0.64 us (1%)
    pallas_call x1, Pallas kernels, on_device(): pl.pallas_call(functools.partial(main_kernel, n_dev, n_sec, pieces), out_...  39.6 us
    pallas_call x1, Pallas kernels, on_device(): pl.pallas_call(down_kernel, grid=(hid // block,), out_shape=(jax.ShapeDty...  9.51 us

profile of v2, /device:TPU:1, one launch (start us, length us, event | category | flops | bytes accessed | tf_op | source)
XLA Modules:
  0.0 49.8 jit_solution(3545918432318251955)
XLA Ops:
  0.6 39.6 %shard_map.86 = (bf16[32,7168]{1,0:T(8,128)(2,1)}, bf16[32,7168]{1,0:T(8,128)(2,1)}, bf16[32,1024]{1,0:T(8,128)(2,1)}) custom-call(bf16[1,32,7168]{2,1,0:T(8,128)(2,1)} %grad_ref.1, s32[1,8,32]{2,1,0:T(8,128)} %bitcast.4, f32[1,8,32]{2,1,0:T(8,128)} %bitcast.5, bf16[1,24,2,1024]{3,2,1,0:T(2,128)(2,1)} %pre_ref.1, bf16[1024,7168]{1,0:T(8,128)(2,1)} %wg_hbm.1, ...), custom_call_target="tpu_custom_call" | custom-call | flops 1409286144 | bytes 44040192 | tf_op jit(solution)/shard_map/pallas_call | solution.py:328
  40.3 9.5 %shard_map.87 = (bf16[1024,7168]{1,0:T(8,128)(2,1)}, bf16[32,7168]{1,0:T(8,128)(2,1)}) custom-call(bf16[32,1024]{1,0:T(8,128)(2,1)} %get-tuple-element.7.hidden_ref, bf16[32,7168]{1,0:T(8,128)(2,1)} %get-tuple-element.8.rows_ref, bf16[32,7168]{1,0:T(8,128)(2,1)} %get-tuple-element.9.passed_ref), custom_call_target="tpu_custom_call" | custom-call | flops 469762048 | bytes 14680064 | tf_op jit(solution)/shard_map/pallas_call | solution.py:370

commit v3 on v2

v3 whole, which is shorter than its diff:
```python
import functools

import jax
import jax.numpy as jnp
from jax import lax
from jax.experimental import pallas as pl
from jax.experimental.pallas import tpu as pltpu
from jax.sharding import PartitionSpec as P

EXPERTS = 4
SLOT = 3
PAD = 4
FOLD = 4
ROWS = EXPERTS * PAD
UNIT = 512
GATHER_PIECES = 3
RETURN_PIECES = 4
F32 = jnp.float32
BF16 = jnp.bfloat16


def nt(a, b):
    return lax.dot_general(a, b, (((1,), (1,)), ((), ())), preferred_element_type=F32)


def tn(a, b):
    return lax.dot_general(a, b, (((0,), (0,)), ((), ())), preferred_element_type=F32)


def nn(a, b):
    return lax.dot_general(a, b, (((1,), (0,)), ((), ())), preferred_element_type=F32)


def split(width, count):
    units = width // UNIT
    sizes = [UNIT * (units // count + (1 if i < units % count else 0)) for i in range(count)]
    return [(sum(sizes[:i]), size) for i, size in enumerate(sizes)]


def iota(shape, dim):
    return lax.broadcasted_iota(jnp.int32, shape, dim)


def main_kernel(
    n_dev, n_sec, gp, rp,
    grad_ref, ids_ref, gates_ref, pre_ref, wg_hbm, wu_hbm, wd_hbm,
    passed_ref, rows_ref, hidden_ref,
    wg, wu, wd, gsend, grecv, xsend, xrecv, zsend, zrecv, gbuf, dh, fg, fu, dgate, dup,
    sel, whi, wlo, perm,
    wd_sem, wg_sem, wu_sem,
    gz_s, gz_r, gx_s, gx_r, rx_s, rx_r, rz_s, rz_r, ps_s, ps_r,
):
    slices = n_dev // EXPERTS
    tok = grad_ref.shape[1]
    j = lax.axis_index("ep")
    s = lax.axis_index("section")
    e = lax.div(j, slices)
    g = lax.rem(j, slices)

    def cols(pc):
        return pl.ds(pc[0], pc[1])

    def narrow(pc):
        return pl.ds(pc[0] // FOLD, pc[1] // FOLD)

    def folded(x, pc):
        w = pc[1] // FOLD
        return jnp.concatenate([x[:, f * w:(f + 1) * w] for f in range(FOLD)], axis=0)

    def unfolded(x, rows):
        return jnp.concatenate([x[f * rows:(f + 1) * rows] for f in range(FOLD)], axis=1)

    def wcopy(hbm, vm, sem, i, pc):
        return pltpu.make_async_copy(hbm.at[:, cols(pc)], vm.at[:, cols(pc)], sem.at[i])

    barrier = pltpu.get_barrier_semaphore()
    for d in range(1, EXPERTS):
        pl.semaphore_signal(barrier, inc=1, device_id={"ep": lax.rem(e + d, EXPERTS) * slices + g},
                            device_id_type=pl.DeviceIdType.MESH)
    for d in range(1, slices):
        pl.semaphore_signal(barrier, inc=1, device_id={"ep": e * slices + lax.rem(g + d, slices)},
                            device_id_type=pl.DeviceIdType.MESH)

    @pl.when(s > 0)
    def _():
        pl.semaphore_signal(barrier, inc=1, device_id={"section": s - 1},
                            device_id_type=pl.DeviceIdType.MESH)

    @pl.when(s < n_sec - 1)
    def _():
        pl.semaphore_signal(barrier, inc=1, device_id={"section": s + 1},
                            device_id_type=pl.DeviceIdType.MESH)

    for i, pc in enumerate(gp):
        wcopy(wd_hbm, wd, wd_sem, i, pc).start()
    for i, pc in enumerate(rp):
        wcopy(wg_hbm, wg, wg_sem, i, pc).start()
        wcopy(wu_hbm, wu, wu_sem, i, pc).start()

    ids = ids_ref[0]
    gates = gates_ref[0]
    q = EXPERTS * FOLD * PAD
    qt = FOLD * tok
    named = iota((ROWS, tok), 0)
    member = jnp.zeros((ROWS, tok), F32)
    coef = jnp.zeros((ROWS, tok), F32)
    for c in range(ids.shape[0]):
        eq = ids[c:c + 1, :] == named
        member = member + jnp.where(eq, 1.0, 0.0)
        coef = coef + jnp.where(eq, gates[c:c + 1, :], 0.0)
    tri = jnp.where(iota((tok, tok), 0) <= iota((tok, tok), 1), 1.0, 0.0).astype(BF16)
    rank = nn(member.astype(BF16), tri) - 1.0
    rank = jnp.where(member == 1.0, rank, -1.0).astype(BF16)
    tile = jnp.where(iota((tok, qt), 0) == lax.rem(iota((tok, qt), 1), tok), 1.0, 0.0).astype(BF16)
    rank4 = nn(rank, tile).astype(BF16)
    spread = jnp.where((iota((q, ROWS), 0) >> 4) == iota((q, ROWS), 1), 1.0, 0.0).astype(BF16)
    spread_t = jnp.where(iota((ROWS, q), 0) == (iota((ROWS, q), 1) >> 4), 1.0, 0.0).astype(BF16)
    ri, rj = iota((q, qt), 0), iota((q, qt), 1)
    hit = jnp.logical_and(
        nn(spread, rank4) == (ri & 3).astype(F32),
        jnp.logical_and(((ri >> 2) & 3) == lax.div(rj, tok), (ri & 3) < SLOT),
    )
    sel[...] = jnp.where(hit, 1.0, 0.0).astype(BF16)
    ci, cj = iota((qt, q), 0), iota((qt, q), 1)
    hit_t = jnp.logical_and(
        tn(rank4, spread_t) == (cj & 3).astype(F32),
        jnp.logical_and(((cj >> 2) & 3) == lax.div(ci, tok), (cj & 3) < SLOT),
    )
    high = coef.astype(BF16)
    low = (coef - high.astype(F32)).astype(BF16)
    high4 = nn(high, tile).astype(BF16)
    low4 = nn(low, tile).astype(BF16)
    whi[...] = jnp.where(hit_t, tn(high4, spread_t), 0.0).astype(BF16)
    wlo[...] = jnp.where(hit_t, tn(low4, spread_t), 0.0).astype(BF16)
    fi, fj = iota((q, q), 0), iota((q, q), 1)
    perm[...] = jnp.where(
        jnp.logical_and(
            jnp.logical_and((fi >> 4) == ((fj >> 2) & 3), ((fi >> 2) & 3) == (fj >> 4)),
            (fi & 3) == (fj & 3),
        ),
        1.0, 0.0,
    ).astype(BF16)

    def block(i):
        return pl.ds(pl.multiple_of(i * ROWS, ROWS), ROWS)

    def z_copy(src, dst, ss, rs, i, pc, d):
        to = lax.rem(e + d, EXPERTS)
        return pltpu.make_async_remote_copy(
            src_ref=src.at[block(to), narrow(pc)], dst_ref=dst.at[block(e), narrow(pc)],
            send_sem=ss.at[i, d - 1], recv_sem=rs.at[i, d - 1],
            device_id={"ep": to * slices + g}, device_id_type=pl.DeviceIdType.MESH)

    def z_wait(src, dst, ss, rs, i, pc, d):
        frm = lax.rem(e + EXPERTS - d, EXPERTS)
        pltpu.make_async_remote_copy(
            src_ref=src.at[block(frm), narrow(pc)], dst_ref=dst.at[block(frm), narrow(pc)],
            send_sem=ss.at[i, d - 1], recv_sem=rs.at[i, d - 1],
            device_id={"ep": frm * slices + g}, device_id_type=pl.DeviceIdType.MESH).wait_recv()

    def gx_copy(i, pc, d, row):
        at = rows_ref.at[block(row), cols(pc)]
        return pltpu.make_async_remote_copy(
            src_ref=at, dst_ref=at, send_sem=gx_s.at[i, d - 1], recv_sem=gx_r.at[i, d - 1],
            device_id={"ep": e * slices + lax.rem(g + d, slices)},
            device_id_type=pl.DeviceIdType.MESH)

    def rx_copy(i, pc, d):
        to = lax.rem(g + d, slices)
        return pltpu.make_async_remote_copy(
            src_ref=xsend.at[block(to), cols(pc)], dst_ref=xrecv.at[d - 1, :, cols(pc)],
            send_sem=rx_s.at[i, d - 1], recv_sem=rx_r.at[i, d - 1],
            device_id={"ep": e * slices + to}, device_id_type=pl.DeviceIdType.MESH)

    def ps_copy(i, pc):
        return pltpu.make_async_remote_copy(
            src_ref=gbuf.at[:, cols(pc)], dst_ref=passed_ref.at[:, cols(pc)],
            send_sem=ps_s.at[i], recv_sem=ps_r.at[i],
            device_id={"section": lax.rem(s + n_sec - 1, n_sec)},
            device_id_type=pl.DeviceIdType.MESH)

    neighbours = lax.div(s + n_sec - 1, n_sec) + lax.div(2 * n_sec - 2 - s, n_sec)
    pl.semaphore_wait(barrier, EXPERTS - 1 + slices - 1 + neighbours)

    for i, pc in enumerate(gp):
        gsend[:, narrow(pc)] = nn(sel[...], folded(grad_ref[0, :, cols(pc)], pc)).astype(BF16)
        for d in range(1, EXPERTS):
            z_copy(gsend, grecv, gz_s, gz_r, i, pc, d).start()
        grecv[block(e), narrow(pc)] = gsend[block(e), narrow(pc)]

    m = slices * ROWS
    r = n_dev * SLOT
    pi, pj = iota((m, r), 0), iota((m, r), 1)
    source = (((pi >> 2) & 3) * slices + (pi >> 4)) * SLOT + (pi & 3)
    order = jnp.where(jnp.logical_and(source == pj, (pi & 3) < SLOT), 1.0, 0.0).astype(BF16)
    a = nn(order, pre_ref[0, :, 0, :])
    u = nn(order, pre_ref[0, :, 1, :])
    sig = jax.nn.sigmoid(a)
    swish = a * sig
    hidden_ref[...] = (swish * u).astype(BF16)
    fg[...] = u * sig * (1.0 + a * (1.0 - sig))
    fu[...] = swish
    dh[...] = jnp.zeros_like(dh)

    @pl.when(s == n_sec - 1)
    def _():
        passed_ref[...] = jnp.zeros_like(passed_ref)

    def take(i, pc):
        for d in range(1, EXPERTS):
            z_wait(gsend, grecv, gz_s, gz_r, i, pc, d)
        flat = nn(perm[...], grecv[:, narrow(pc)]).astype(BF16)
        rows_ref[block(g), cols(pc)] = unfolded(flat, ROWS)
        for d in range(1, slices):
            gx_copy(i, pc, d, g).start()

    def project(i, pc):
        for d in range(1, slices):
            gx_copy(i, pc, d, lax.rem(g + slices - d, slices)).wait_recv()
        wcopy(wd_hbm, wd, wd_sem, i, pc).wait()
        dh[...] += nt(rows_ref[:, cols(pc)], wd[:, cols(pc)])

    lag = 2
    for i in range(len(gp) + lag):
        if i < len(gp):
            take(i, gp[i])
        if i >= lag:
            project(i - lag, gp[i - lag])

    d_hidden = dh[...]
    dgate[...] = (d_hidden * fg[...]).astype(BF16)
    dup[...] = (d_hidden * fu[...]).astype(BF16)

    def multiply(i, pc):
        wcopy(wg_hbm, wg, wg_sem, i, pc).wait()
        wcopy(wu_hbm, wu, wu_sem, i, pc).wait()
        total = nn(dgate[...], wg[:, cols(pc)]) + nn(dup[...], wu[:, cols(pc)])
        xsend[:, cols(pc)] = total.astype(BF16)
        for d in range(1, slices):
            rx_copy(i, pc, d).start()

    def add_pair(i, pc):
        acc = xsend[block(g), cols(pc)].astype(F32)
        for d in range(1, slices):
            rx_copy(i, pc, d).wait_recv()
            acc = acc + xrecv[d - 1, :, cols(pc)].astype(F32)
        zsend[:, narrow(pc)] = nn(perm[...], folded(acc.astype(BF16), pc)).astype(BF16)
        for d in range(1, EXPERTS):
            z_copy(zsend, zrecv, rz_s, rz_r, i, pc, d).start()
        zrecv[block(e), narrow(pc)] = zsend[block(e), narrow(pc)]

    def combine(i, pc):
        for d in range(1, EXPERTS):
            z_wait(zsend, zrecv, rz_s, rz_r, i, pc, d)
        got = zrecv[:, narrow(pc)]
        terms = nn(whi[...], got) + nn(wlo[...], got)
        gbuf[:, cols(pc)] = (grad_ref[0, :, cols(pc)].astype(F32) + unfolded(terms, tok)).astype(BF16)

        @pl.when(s > 0)
        def _():
            ps_copy(i, pc).start()

    lag_x, lag_z = 1, 3
    for i in range(len(rp) + lag_z):
        if i < len(rp):
            multiply(i, rp[i])
        if lag_x <= i < len(rp) + lag_x:
            add_pair(i - lag_x, rp[i - lag_x])
        if i >= lag_z:
            combine(i - lag_z, rp[i - lag_z])

    for i, pc in enumerate(gp):
        for d in range(1, EXPERTS):
            z_copy(gsend, grecv, gz_s, gz_r, i, pc, d).wait_send()
        for d in range(1, slices):
            gx_copy(i, pc, d, g).wait_send()
    for i, pc in enumerate(rp):
        for d in range(1, EXPERTS):
            z_copy(zsend, zrecv, rz_s, rz_r, i, pc, d).wait_send()
        for d in range(1, slices):
            rx_copy(i, pc, d).wait_send()

    @pl.when(s < n_sec - 1)
    def _():
        for i, pc in enumerate(rp):
            ps_copy(i, pc).wait_recv()

    @pl.when(s > 0)
    def _():
        for i, pc in enumerate(rp):
            ps_copy(i, pc).wait_send()


def down_kernel(hidden_ref, rows_ref, passed_ref, down_ref, out_ref):
    @pl.when(pl.program_id(0) == 0)
    def _():
        out_ref[...] = passed_ref[...]

    step = 2 * UNIT
    h = hidden_ref[...]
    for c in range(rows_ref.shape[1] // step):
        down_ref[:, c * step:(c + 1) * step] = tn(h, rows_ref[:, c * step:(c + 1) * step]).astype(BF16)


def on_device(grad, ids, gates, pre, w_gate, w_up, w_down):
    n_dev = lax.axis_size("ep")
    n_sec = lax.axis_size("section")
    slices = n_dev // EXPERTS
    tok, width = grad.shape[1:]
    hid = w_down.shape[0]
    gp, rp = split(width, GATHER_PIECES), split(width, RETURN_PIECES)
    g_n, r_n = len(gp), len(rp)
    m = slices * ROWS
    q = EXPERTS * FOLD * PAD
    qt = FOLD * tok
    vmem = pl.BlockSpec(memory_space=pltpu.VMEM)
    hbm = pl.BlockSpec(memory_space=pl.ANY)
    dma = pltpu.SemaphoreType.DMA
    x_n = slices - 1
    z_n = EXPERTS - 1
    passed, rows, hidden = pl.pallas_call(
        functools.partial(main_kernel, n_dev, n_sec, gp, rp),
        out_shape=(
            jax.ShapeDtypeStruct((tok, width), BF16),
            jax.ShapeDtypeStruct((m, width), BF16),
            jax.ShapeDtypeStruct((m, hid), BF16),
        ),
        in_specs=[vmem, vmem, vmem, vmem, hbm, hbm, hbm],
        out_specs=(vmem, vmem, vmem),
        scratch_shapes=[
            pltpu.VMEM((hid, width), BF16),
            pltpu.VMEM((hid, width), BF16),
            pltpu.VMEM((hid, width), BF16),
            pltpu.VMEM((q, width // FOLD), BF16),
            pltpu.VMEM((q, width // FOLD), BF16),
            pltpu.VMEM((m, width), BF16),
            pltpu.VMEM((x_n, ROWS, width), BF16),
            pltpu.VMEM((q, width // FOLD), BF16),
            pltpu.VMEM((q, width // FOLD), BF16),
            pltpu.VMEM((tok, width), BF16),
            pltpu.VMEM((m, hid), F32),
            pltpu.VMEM((m, hid), F32),
            pltpu.VMEM((m, hid), F32),
            pltpu.VMEM((m, hid), BF16),
            pltpu.VMEM((m, hid), BF16),
            pltpu.VMEM((q, qt), BF16),
            pltpu.VMEM((qt, q), BF16),
            pltpu.VMEM((qt, q), BF16),
            pltpu.VMEM((q, q), BF16),
            dma((g_n,)), dma((r_n,)), dma((r_n,)),
            dma((g_n, z_n)), dma((g_n, z_n)),
            dma((g_n, x_n)), dma((g_n, x_n)),
            dma((r_n, x_n)), dma((r_n, x_n)),
            dma((r_n, z_n)), dma((r_n, z_n)),
            dma((r_n,)), dma((r_n,)),
        ],
        compiler_params=pltpu.CompilerParams(
            collective_id=0, has_side_effects=True, vmem_limit_bytes=60 * 1024 * 1024),
        cost_estimate=pl.CostEstimate(
            flops=6 * m * hid * width, bytes_accessed=6 * hid * width, transcendentals=m * hid),
    )(grad, jnp.swapaxes(ids, 1, 2), jnp.swapaxes(gates, 1, 2), pre, w_gate, w_up, w_down)
    block = min(hid, 256)
    down, out = pl.pallas_call(
        down_kernel,
        grid=(hid // block,),
        out_shape=(
            jax.ShapeDtypeStruct((hid, width), BF16),
            jax.ShapeDtypeStruct((tok, width), BF16),
        ),
        in_specs=[
            pl.BlockSpec((m, block), lambda i: (0, i)),
            pl.BlockSpec((m, width), lambda i: (0, 0)),
            pl.BlockSpec((tok, width), lambda i: (0, 0)),
        ],
        out_specs=(
            pl.BlockSpec((block, width), lambda i: (i, 0)),
            pl.BlockSpec((tok, width), lambda i: (0, 0)),
        ),
        compiler_params=pltpu.CompilerParams(vmem_limit_bytes=60 * 1024 * 1024),
        cost_estimate=pl.CostEstimate(
            flops=2 * m * hid * width, bytes_accessed=2 * hid * width, transcendentals=0),
    )(hidden, rows, passed)
    return (out[None], down[None])


def solution(mesh):
    placed = (
        P("section", "ep", None),
        P("section", "ep", None),
        P("section", "ep", None),
        P("section", "ep", None, None),
        P("ep", None),
        P("ep", None),
        P("ep", None),
    )
    return jax.shard_map(
        on_device,
        mesh=mesh,
        in_specs=placed,
        out_specs=(P("section", "ep", None), P("section", "ep", None)),
        check_vma=False,
    )
```

time: 50.1 us -> 48.8 us (0.974)
  Pallas kernels: 49.1 us -> 48 us
    pallas_call x1, Pallas kernels: 9.51 us -> 8.42 us  [on_device(): pl.pallas_call(down_kernel, grid=(hid // block,), out_shape=(jax.ShapeDty...]
where the time goes in v3:
time: 48.8 us; the launch traced here: 48.6 us
  Pallas kernels  48 us (98%)
  between operations  0.64 us (1%)
    pallas_call x1, Pallas kernels, on_device(): pl.pallas_call(functools.partial(main_kernel, n_dev, n_sec, gp, rp), out_...  39.6 us
    pallas_call x1, Pallas kernels, on_device(): pl.pallas_call(down_kernel, grid=(hid // block,), out_shape=(jax.ShapeDty...  8.42 us

profile of v3, /device:TPU:1, one launch (start us, length us, event | category | flops | bytes accessed | tf_op | source)
XLA Modules:
  0.0 48.6 jit_solution(13944618450374755323)
XLA Ops:
  0.6 39.6 %shard_map.86 = (bf16[32,7168]{1,0:T(8,128)(2,1)}, bf16[32,7168]{1,0:T(8,128)(2,1)}, bf16[32,1024]{1,0:T(8,128)(2,1)}) custom-call(bf16[1,32,7168]{2,1,0:T(8,128)(2,1)} %grad_ref.1, s32[1,8,32]{2,1,0:T(8,128)} %bitcast.4, f32[1,8,32]{2,1,0:T(8,128)} %bitcast.5, bf16[1,24,2,1024]{3,2,1,0:T(2,128)(2,1)} %pre_ref.1, bf16[1024,7168]{1,0:T(8,128)(2,1)} %wg_hbm.1, ...), custom_call_target="tpu_custom_call" | custom-call | flops 1409286144 | bytes 44040192 | tf_op jit(solution)/shard_map/pallas_call | solution.py:321
  40.2 8.4 %shard_map.87 = (bf16[1024,7168]{1,0:T(8,128)(2,1)}, bf16[32,7168]{1,0:T(8,128)(2,1)}) custom-call(bf16[32,1024]{1,0:T(8,128)(2,1)} %get-tuple-element.7.hidden_ref, bf16[32,7168]{1,0:T(8,128)(2,1)} %get-tuple-element.8.rows_ref, bf16[32,7168]{1,0:T(8,128)(2,1)} %get-tuple-element.9.passed_ref), custom_call_target="tpu_custom_call" | custom-call | flops 469762048 | bytes 14680064 | tf_op jit(solution)/shard_map/pallas_call | solution.py:363
